TPU v7x, 32 devices: a whole 2x2x4 slice. The times are simulated.
32 devices in a mesh: offset: 2 (over x), inline: 4 (over z), tm: 4 (over y, core).
Axes of the slice: x: 2, y: 2, z: 4, core: 2. Of those that a mesh axis runs over, the one named last changes fastest.
Arguments:
- traces: float32 [2, 32, 16, 2048], P('offset', 'inline', None, 'tm'), may hold values from -6 to 6
- class_of_block: int32 [2], P('offset'), may hold values from 0 to 15, as said below
- band_start: int32 [16, 5, 2048], P(None, None, 'tm'), may hold values from 0 to 121
- band_weights: float32 [16, 5, 8, 2048], P(None, None, None, 'tm'), may hold values from -1 to 1
Outputs:
- migrated: float32 [32, 16, 2048], P('inline', None, 'tm')
- residual: float32 [2, 32, 16, 2048], P('offset', 'inline', None, 'tm')
Inputs may be any that keep to these rules, and one draw needn't show every extreme that they name: band_start[c, a, t] is the smallest delay of the band that data time t reads from the image at aperture distance a - 2; the band's delays are band_start[c, a, t] + k for k below 8. `class_of_block`: the first min(2, 16) blocks have different classes, and class 16 - 1 is among them.
All inputs are finite; a program needn't handle non-finite values.
Results may differ from a plain program's by a relative error of at most 0.0003.
Values sent between devices are 32-bit elements; how exact they have to be, the bound alone decides.
A program may use at most 64 MiB of HBM per device.

v0:
```python
import functools

import jax
import jax.numpy as jnp
from jax import lax
from jax.experimental import pallas as pl
from jax.experimental.pallas import tpu as pltpu
from jax.sharding import PartitionSpec as P

K = 8
LAG = 128
APER = 2
ITERS = 2


def with_halo(block, sides, width):
    for axis, dim in sides:
        count = lax.axis_size(axis)
        forward = [(i, i + 1) for i in range(count - 1)]
        backward = [(target, source) for source, target in forward]
        low = lax.ppermute(
            lax.slice_in_dim(block, block.shape[dim] - width, None, axis=dim), axis, forward
        )
        high = lax.ppermute(lax.slice_in_dim(block, 0, width, axis=dim), axis, backward)
        block = jnp.concatenate([low, block, high], axis=dim)
    return block


def shifted(shard, axis, by):
    count = lax.axis_size(axis)
    pairs = [(i, i + by) for i in range(count) if 0 <= i + by < count]
    return lax.ppermute(shard, axis, pairs)


def widen_inline(field):
    return with_halo(field, (("inline", 1),), APER)


def totalled(value):
    return lax.psum(value, ("offset", "inline", "tm"))


def on_device_general(traces, class_of_block, band_start, band_weights):
    own_class = class_of_block[0]
    weights = lax.dynamic_index_in_dim(band_weights, own_class, 0, keepdims=False)
    starts = lax.dynamic_index_in_dim(band_start, own_class, 0, keepdims=False)
    inlines = traces.shape[1]
    crosslines = traces.shape[2]
    window = traces.shape[3]
    flat_rows = inlines * crosslines
    sample_rows = jnp.arange(window, dtype=jnp.int32)[:, None]
    sample_cols = jnp.arange(window + LAG, dtype=jnp.int32)[None, :]
    band_list = []
    for aper_index in range(2 * APER + 1):
        band_matrix = jnp.zeros((window, window + LAG), jnp.float32)
        for tap_index in range(K):
            target = sample_rows - starts[aper_index][:, None] - tap_index + LAG
            band_matrix = band_matrix + jnp.where(
                sample_cols == target, weights[aper_index, tap_index][:, None], 0.0
            )
        band_list.append(band_matrix)

    def migrate_block(values):
        widened = widen_inline(values)[0]
        result_sum = jnp.zeros((flat_rows, window + LAG), jnp.float32)
        for aper_index in range(2 * APER + 1):
            first = 2 * APER - aper_index
            slab_rows = widened[first : first + inlines].reshape(flat_rows, window)
            result_sum = result_sum + jnp.dot(
                slab_rows,
                band_list[aper_index],
                precision=lax.Precision.HIGHEST,
                preferred_element_type=jnp.float32,
            )
        result_sum = result_sum.reshape(inlines, crosslines, window + LAG)
        later_part = shifted(result_sum[:, :, :LAG], "tm", -1)
        own_part = result_sum[:, :, LAG:]
        return own_part.at[:, :, window - LAG :].add(later_part)

    def migrate(values):
        partial_image = migrate_block(values)
        gradient = lax.psum(partial_image, "offset")
        grad_norm = totalled(jnp.sum(gradient * gradient)) / lax.axis_size("offset")
        return (gradient, grad_norm)

    migrated = jnp.zeros((inlines, crosslines, window), jnp.float32)
    residual = traces
    gradient, grad_norm = migrate(residual)
    direction = gradient
    for iteration in range(ITERS):
        demigrate_widened = widen_inline(direction[None])[0]
        earlier = shifted(demigrate_widened[:, :, window - LAG :], "tm", 1)
        full_block = jnp.concatenate([earlier, demigrate_widened], axis=2)
        demigrate_result_sum = jnp.zeros((flat_rows, window), jnp.float32)
        for demigrate_aper_index in range(2 * APER + 1):
            demigrate_slab_rows = full_block[
                demigrate_aper_index : demigrate_aper_index + inlines
            ].reshape(flat_rows, window + LAG)
            demigrate_result_sum = demigrate_result_sum + lax.dot_general(
                demigrate_slab_rows,
                band_list[demigrate_aper_index],
                (((1,), (1,)), ((), ())),
                precision=lax.Precision.HIGHEST,
                preferred_element_type=jnp.float32,
            )
        projected = demigrate_result_sum.reshape(1, inlines, crosslines, window)
        curvature = totalled(jnp.sum(projected * projected))
        step_size = grad_norm / curvature
        migrated = migrated + step_size * direction
        residual = residual - step_size * projected
        if iteration + 1 < ITERS:
            gradient, grad_new = migrate(residual)
            direction = gradient + grad_new / grad_norm * direction
            grad_norm = grad_new
    return (migrated, residual)


TB = 128
MESH = pl.DeviceIdType.MESH
NAPER = 2 * APER + 1


def kernel(
    n_in, n_tm,
    cls_ref, tr_ref, st_ref, w_ref, mig_ref, res_ref,
    vt, p0, p1, ext, prev_strip, next_strip, img, bh, bl, cl, sa, sb, mg, px,
    local_sem, send_sem, recv_sem,
):
    o = lax.axis_index("offset")
    i = lax.axis_index("inline")
    t = lax.axis_index("tm")
    other = 1 - o
    rows, window = tr_ref.shape[1], tr_ref.shape[3]
    xl = tr_ref.shape[2] // 2
    tiles = window // TB
    flat = rows * xl
    own_x = pl.ds(pl.multiple_of(o * xl, xl), xl)
    other_x = pl.ds(pl.multiple_of(other * xl, xl), xl)
    plane = 2 * n_tm
    m = o * n_tm + t

    barrier = pltpu.get_barrier_semaphore()
    greeted = []
    for d in range(1, plane):
        peer = lax.rem(m + d, plane)
        greeted.append((lax.div(peer, n_tm), i, lax.rem(peer, n_tm)))
    for d in range(1, n_in):
        greeted.append((o, lax.rem(i + d, n_in), t))
    for di in sorted({1 % n_in, n_in - 1} - {0}):
        greeted.append((other, lax.rem(i + di, n_in), t))
        for dt in sorted({1 % n_tm, n_tm - 1} - {0}):
            greeted.append((o, lax.rem(i + di, n_in), lax.rem(t + dt, n_tm)))
    for device in greeted:
        pl.semaphore_signal(barrier, inc=1, device_id=device, device_id_type=MESH)
    pl.semaphore_wait(barrier, len(greeted))

    used = [0]

    def both(first, second):
        if first is None:
            return second
        if second is None:
            return first
        return jnp.logical_and(first, second)

    def inside(index, step, count):
        if step == 0:
            return None
        if step > 0:
            return index + step < count
        return index + step >= 0

    def guarded(condition, action):
        if condition is None:
            action()
        else:
            pl.when(condition)(action)

    class Message:
        def __init__(self, src, dst, device, can_send=None, can_receive=None):
            number = used[0]
            used[0] += 1
            self.copy = pltpu.make_async_remote_copy(
                src_ref=src, dst_ref=dst,
                send_sem=send_sem.at[number], recv_sem=recv_sem.at[number],
                device_id=device, device_id_type=MESH,
            )
            self.can_send, self.can_receive = can_send, can_receive
            guarded(can_send, self.copy.start)

        def received(self):
            guarded(self.can_receive, self.copy.wait_recv)

        def sent(self):
            guarded(self.can_send, self.copy.wait_send)

    pending = []

    def send(*args):
        message = Message(*args)
        pending.append(message)
        return message

    def neighbour(src, dst, di, dt, do=0):
        return send(
            src, dst, (o if do == 0 else other, i + di, t + dt),
            both(inside(i, di, n_in), inside(t, dt, n_tm)),
            both(inside(i, -di, n_in), inside(t, -dt, n_tm)),
        )

    lo_halo, hi_halo = pl.ds(0, APER), pl.ds(APER + rows, APER)
    body = pl.ds(APER, rows)
    first_rows, last_rows = pl.ds(APER, APER), pl.ds(rows, APER)

    cl[0] = jnp.full(cl.shape[1:], cls_ref[0], jnp.int32)
    class_msg = send(cl.at[0], cl.at[1], (other, i, t))
    entry = []
    for slot, xs in ((1, other_x), (0, own_x)):
        entry.append(neighbour(tr_ref.at[0, pl.ds(0, APER), xs], vt.at[slot, hi_halo], -1, 0, slot))
        entry.append(neighbour(tr_ref.at[0, pl.ds(rows - APER, APER), xs], vt.at[slot, lo_halo], 1, 0, slot))
    entry.append(send(tr_ref.at[0, :, other_x], vt.at[1, body], (other, i, t)))
    own_copy = pltpu.make_async_copy(tr_ref.at[0, :, own_x], vt.at[0, body], local_sem)
    own_copy.start()

    @pl.when(i == 0)
    def _():
        vt[:, 0:APER] = jnp.zeros_like(vt[:, 0:APER])
        p0[:, 0:APER] = jnp.zeros_like(p0[:, 0:APER])
        for u in range(2):
            ext[u, 0:APER] = jnp.zeros_like(ext[u, 0:APER])
            prev_strip[u, 0:APER] = jnp.zeros_like(prev_strip[u, 0:APER])
            next_strip[u, 0:APER] = jnp.zeros_like(next_strip[u, 0:APER])

    @pl.when(i == n_in - 1)
    def _():
        top = slice(APER + rows, 2 * APER + rows)
        vt[:, top] = jnp.zeros_like(vt[:, top])
        p0[:, top] = jnp.zeros_like(p0[:, top])
        for u in range(2):
            ext[u, top] = jnp.zeros_like(ext[u, top])
            prev_strip[u, top] = jnp.zeros_like(prev_strip[u, top])
            next_strip[u, top] = jnp.zeros_like(next_strip[u, top])

    @pl.when(jnp.logical_and(t == 0, i >= 0))
    def _():
        prev_strip[:, APER:APER + rows] = jnp.zeros_like(prev_strip[:, APER:APER + rows])

        @pl.when(i > 0)
        def _():
            prev_strip[:, 0:APER] = jnp.zeros_like(prev_strip[:, 0:APER])

        @pl.when(i < n_in - 1)
        def _():
            top = slice(APER + rows, 2 * APER + rows)
            prev_strip[:, top] = jnp.zeros_like(prev_strip[:, top])

    @pl.when(t == n_tm - 1)
    def _():
        next_strip[:, APER:APER + rows] = jnp.zeros_like(next_strip[:, APER:APER + rows])

        @pl.when(i > 0)
        def _():
            next_strip[:, 0:APER] = jnp.zeros_like(next_strip[:, 0:APER])

        @pl.when(i < n_in - 1)
        def _():
            top = slice(APER + rows, 2 * APER + rows)
            next_strip[:, top] = jnp.zeros_like(next_strip[:, top])

    sub = lax.broadcasted_iota(jnp.int32, (K, TB), 0)
    lane = lax.broadcasted_iota(jnp.int32, (K, TB), 1)
    groups = lax.broadcasted_iota(jnp.int32, (2 * TB // K, K, TB), 0)

    def build(slot):
        masks = [cl[slot] == c for c in range(st_ref.shape[0])]

        def one(j, carry):
            cols = pl.ds(pl.multiple_of(j * TB, TB), TB)
            for a in range(NAPER):
                start = jnp.zeros((K, TB), jnp.int32)
                taps = jnp.zeros((K, TB), jnp.float32)
                for c, mask in enumerate(masks):
                    row = jnp.broadcast_to(st_ref[c, a:a + 1, cols], (K, TB))
                    start = jnp.where(mask, row, start)
                    taps = jnp.where(mask, w_ref[c, a, :, cols], taps)
                reach = lane + LAG - start - sub
                group = lax.shift_right_logical(reach, 3)
                tap = jnp.bitwise_and(reach, K - 1)
                turned = jnp.zeros((K, TB), jnp.float32)
                for k in range(K):
                    turned = jnp.where(tap == k, jnp.broadcast_to(taps[k:k + 1], (K, TB)), turned)
                high = turned.astype(jnp.bfloat16).astype(jnp.float32)
                low = turned - high
                hit = groups == group[None]
                place = slice(slot * TB, (slot + 1) * TB)
                bh[a, j, :, place] = jnp.where(hit, high[None], 0.0).reshape(2 * TB, TB).astype(jnp.bfloat16)
                bl[a, j, :, place] = jnp.where(hit, low[None], 0.0).reshape(2 * TB, TB).astype(jnp.bfloat16)
            return carry

        lax.fori_loop(0, tiles, one, 0)

    build(0)
    class_msg.received()
    build(1)
    own_copy.wait()
    for message in entry:
        message.received()

    def apply(data, firsts, j, dims):
        high = data.astype(jnp.bfloat16).astype(jnp.float32)
        low = data - high
        total = None
        for a in range(NAPER):
            r0 = firsts[a]
            slab_high = high[r0:r0 + rows].reshape(flat, 2 * TB)
            slab_low = low[r0:r0 + rows].reshape(flat, 2 * TB)
            stacked = jnp.concatenate([slab_high, slab_low], axis=0).astype(jnp.bfloat16)
            main = lax.dot_general(stacked, bh[a, j], dims, preferred_element_type=jnp.float32)
            rest = lax.dot_general(
                slab_high.astype(jnp.bfloat16), bl[a, j], dims, preferred_element_type=jnp.float32
            )
            term = main[:flat] + (main[flat:] + rest)
            total = term if total is None else total + term
        return total

    def migrate(values, u):
        carried = None
        for j in range(tiles):
            cols = slice(j * TB, (j + 1) * TB)
            data = jnp.concatenate([values[0, :, :, cols], values[1, :, :, cols]], axis=2)
            part = apply(data, [2 * APER - a for a in range(NAPER)], j, (((1,), (1,)), ((), ())))
            head = part[:, :TB] if carried is None else part[:, :TB] + carried
            ext[u, APER:APER + rows, :, cols] = head.reshape(rows, xl, TB)
            carried = part[:, TB:]
        ext[u, APER:APER + rows, :, window:window + TB] = carried.reshape(rows, xl, TB)

    def demigrate(u, store):
        for j in range(tiles):
            data = img[u, :, :, j * TB:(j + 2) * TB]
            part = apply(data, list(range(NAPER)), j, (((1,), (0,)), ((), ())))
            store(j, part.reshape(rows, xl, 2 * TB))

    def swap_edges(u):
        messages = []
        for source, target, di in ((first_rows, hi_halo, -1), (last_rows, lo_halo, 1)):
            messages.append(neighbour(ext.at[u, source], ext.at[u, target], di, 0))
            messages.append(neighbour(
                ext.at[u, source, :, pl.ds(0, TB)], next_strip.at[u, target], di, -1))
            messages.append(neighbour(
                ext.at[u, source, :, pl.ds(window, TB)], prev_strip.at[u, target], di, 1))
        messages.append(neighbour(
            ext.at[u, body, :, pl.ds(0, TB)], next_strip.at[u, body], 0, -1))
        messages.append(neighbour(
            ext.at[u, body, :, pl.ds(window, TB)], prev_strip.at[u, body], 0, 1))
        for message in messages:
            message.received()

    def whole(u):
        earlier = ext[u, :, :, :TB] + prev_strip[u]
        earlier = jnp.where(t == 0, jnp.zeros_like(earlier), earlier)
        return [
            (slice(0, TB), earlier),
            (slice(TB, window), ext[u, :, :, TB:window]),
            (slice(window, window + TB), ext[u, :, :, window:] + next_strip[u]),
        ]

    def tile_sum(value):
        value = value.reshape(-1, xl, window)
        folded = sum(value[:, :, c * TB:(c + 1) * TB] for c in range(tiles))
        return jnp.sum(folded, axis=0)

    def start_total(turn, parts):
        for n, part in enumerate(parts):
            sa[turn, m, n] = part
        messages = []
        for d in range(1, plane):
            peer = lax.rem(m + d, plane)
            messages.append(send(
                sa.at[turn, m], sa.at[turn, m], (lax.div(peer, n_tm), i, lax.rem(peer, n_tm))))
        return messages

    def next_total(turn, messages):
        for message in messages:
            message.received()
        sb[turn, i] = sum(sa[turn, s] for s in range(plane))
        return [
            send(sb.at[turn, i], sb.at[turn, i], (o, lax.rem(i + d, n_in), t))
            for d in range(1, n_in)
        ]

    def end_total(turn, messages):
        for message in messages:
            message.received()
        total = sum(sb[turn, s] for s in range(n_in))
        return [
            jnp.sum(jnp.sum(total[n], axis=1, keepdims=True), axis=0, keepdims=True)
            for n in range(total.shape[0])
        ]

    def own_image(u):
        return img[u, APER:APER + rows, :, LAG:]

    migrate(vt, 0)
    swap_edges(0)
    for cols, value in whole(0):
        img[0, :, :, cols] = value
    mg0_msg = send(img.at[0, body, :, pl.ds(LAG, window)], mg.at[0], (other, i, t))

    def store_p0(j, part):
        for slot in range(2):
            p0[slot, APER:APER + rows, :, j * TB:(j + 1) * TB] = part[:, :, slot * TB:(slot + 1) * TB]

    demigrate(0, store_p0)
    halo = [
        neighbour(p0.at[:, first_rows], p0.at[:, hi_halo], -1, 0),
        neighbour(p0.at[:, last_rows], p0.at[:, lo_halo], 1, 0),
    ]
    own_p0 = p0[:, APER:APER + rows]
    zero_tile = jnp.zeros((xl, TB), jnp.float32)
    messages = start_total(0, [tile_sum(own_image(0) * own_image(0)), tile_sum(own_p0 * own_p0), zero_tile])
    px0_msg = send(p0.at[1, body], px.at[0], (other, i, t))
    for message in halo:
        message.received()
    messages = next_total(0, messages)
    migrate(p0, 1)
    swap_edges(1)
    gnorm, curvature, _ = end_total(0, messages)
    step0 = gnorm / curvature
    for cols, value in whole(1):
        img[1, :, :, cols] = img[0, :, :, cols] - step0[None] * value
    mg1_msg = send(img.at[1, body, :, pl.ds(LAG, window)], mg.at[1], (other, i, t))

    def store_p1(j, part):
        for slot in range(2):
            p1[slot, :, :, j * TB:(j + 1) * TB] = part[:, :, slot * TB:(slot + 1) * TB]

    demigrate(1, store_p1)
    px1_msg = send(p1.at[1], px.at[1], (other, i, t))
    own_p0 = p0[:, APER:APER + rows]
    own_p1 = p1[...]
    messages = start_total(1, [
        tile_sum(own_image(1) * own_image(1)), tile_sum(own_p1 * own_p1), tile_sum(own_p1 * own_p0)])
    messages = next_total(1, messages)
    gnew, square, cross = end_total(1, messages)
    beta = gnew / gnorm
    step1 = gnew / (square + 2.0 * beta * cross + beta * beta * curvature)
    step0, step1, beta = step0[None], step1[None], beta[None]

    def image_of(g0, g1):
        return step0 * g0 + step1 * (g1 + beta * g0)

    def residual_of(r0, a0, a1):
        return r0 - step0 * a0 - step1 * (a1 + beta * a0)

    mig_ref[:, own_x, :] = image_of(own_image(0), own_image(1))
    res_ref[0, :, own_x, :] = residual_of(tr_ref[0, :, own_x, :], p0[0, APER:APER + rows], p1[0])
    for message in (mg0_msg, px0_msg, mg1_msg, px1_msg):
        message.received()
    mig_ref[:, other_x, :] = image_of(mg[0], mg[1])
    res_ref[0, :, other_x, :] = residual_of(tr_ref[0, :, other_x, :], px[0], px[1])
    for message in pending:
        message.sent()


def on_device_pair(n_in, n_tm, traces, class_of_block, band_start, band_weights):
    rows, crosslines, window = traces.shape[1:]
    xl = crosslines // 2
    wide = rows + 2 * APER
    tiles = window // TB
    messages = 64
    f32 = jnp.float32
    vmem = pl.BlockSpec(memory_space=pltpu.VMEM)
    return pl.pallas_call(
        functools.partial(kernel, n_in, n_tm),
        out_shape=(
            jax.ShapeDtypeStruct((rows, crosslines, window), f32),
            jax.ShapeDtypeStruct((1, rows, crosslines, window), f32),
        ),
        in_specs=[pl.BlockSpec(memory_space=pltpu.SMEM), vmem, vmem, vmem],
        out_specs=(vmem, vmem),
        scratch_shapes=[
            pltpu.VMEM((2, wide, xl, window), f32),
            pltpu.VMEM((2, wide, xl, window), f32),
            pltpu.VMEM((2, rows, xl, window), f32),
            pltpu.VMEM((2, wide, xl, window + LAG), f32),
            pltpu.VMEM((2, wide, xl, TB), f32),
            pltpu.VMEM((2, wide, xl, TB), f32),
            pltpu.VMEM((2, wide, xl, window + LAG), f32),
            pltpu.VMEM((NAPER, tiles, 2 * TB, 2 * TB), jnp.bfloat16),
            pltpu.VMEM((NAPER, tiles, 2 * TB, 2 * TB), jnp.bfloat16),
            pltpu.VMEM((2, K, TB), jnp.int32),
            pltpu.VMEM((2, 2 * n_tm, 3, xl, TB), f32),
            pltpu.VMEM((2, n_in, 3, xl, TB), f32),
            pltpu.VMEM((2, rows, xl, window), f32),
            pltpu.VMEM((2, rows, xl, window), f32),
            pltpu.SemaphoreType.DMA,
            pltpu.SemaphoreType.DMA((messages,)),
            pltpu.SemaphoreType.DMA((messages,)),
        ],
        compiler_params=pltpu.CompilerParams(
            collective_id=0, has_side_effects=True, vmem_limit_bytes=40 * 1024 * 1024
        ),
    )(class_of_block, traces, band_start, band_weights)


def solution(mesh):
    placed = (
        P("offset", "inline", None, "tm"),
        P("offset"),
        P(None, None, "tm"),
        P(None, None, None, "tm"),
    )
    if mesh.shape["offset"] == 2:
        body = functools.partial(on_device_pair, mesh.shape["inline"], mesh.shape["tm"])
    else:
        body = on_device_general
    return jax.shard_map(
        body,
        mesh=mesh,
        in_specs=placed,
        out_specs=(P("inline", None, "tm"), P("offset", "inline", None, "tm")),
        check_vma=False,
    )
```

profile of v0, /device:TPU:0, one launch (start us, length us, event | category | flops | bytes accessed | tf_op | source)
XLA Modules:
  0.0 47.4 jit_solution(4540065593011766782)
XLA Ops:
  1.3 1.0 %copy.6.st_ref = s32[16,5,512]{2,1,0:T(8,128)S(1)} copy(s32[16,5,512]{2,0,1:T(8,128)} %param.6) | data formatting | bytes 327680 | tf_op args[2]
  2.3 0.0 copy-start
  2.3 1.3 %copy-done = f32[16,5,8,512]{3,2,1,0:T(8,128)S(1)} copy-done((f32[16,5,8,512]{3,2,1,0:T(8,128)S(1)}, f32[16,5,8,512]{3,2,1,0:T(8,128)}, u32[]{:S(2)}) %copy-start) | copy-done | bytes 1310744
  3.6 0.0 copy-start.1
  3.6 0.9 %copy-done.1 = f32[1,8,16,512]{3,2,1,0:T(8,128)S(1)} copy-done((f32[1,8,16,512]{3,2,1,0:T(8,128)S(1)}, f32[1,8,16,512]{3,2,1,0:T(8,128)}, u32[]{:S(2)}) %copy-start.1) | copy-done | bytes 262168
  4.6 41.4 %shard_map.59 = (f32[8,16,512]{2,1,0:T(8,128)S(1)}, f32[1,8,16,512]{3,2,1,0:T(8,128)S(1)}) custom-call(s32[1]{0:T(128)S(6)} %copy.9.cls_ref, f32[1,8,16,512]{3,2,1,0:T(8,128)S(1)} %copy-done.1, s32[16,5,512]{2,1,0:T(8,128)S(1)} %copy.6.st_ref, f32[16,5,8,512]{3,2,1,0:T(8,128)S(1)} %copy-done), custom_call_target="tpu_custom_call" | custom-call | tf_op jit(solution)/shard_map/pallas_call | solution.py:473
  46.0 0.7 %copy.10 = f32[8,16,512]{2,1,0:T(8,128)} copy(f32[8,16,512]{2,1,0:T(8,128)S(1)} %get-tuple-element.4) | data formatting | bytes 524288
  46.7 0.7 %copy.11 = f32[1,8,16,512]{3,2,1,0:T(8,128)} copy(f32[1,8,16,512]{3,2,1,0:T(8,128)S(1)} %get-tuple-element.5) | data formatting | bytes 524288
Async XLA Ops:
  2.3 1.3 %copy-start = (f32[16,5,8,512]{3,2,1,0:T(8,128)S(1)}, f32[16,5,8,512]{3,2,1,0:T(8,128)}, u32[]{:S(2)}) copy-start(f32[16,5,8,512]{3,2,1,0:T(8,128)} %w_ref.1) | copy-start | bytes 3932164
  3.6 0.9 %copy-start.1 = (f32[1,8,16,512]{3,2,1,0:T(8,128)S(1)}, f32[1,8,16,512]{3,2,1,0:T(8,128)}, u32[]{:S(2)}) copy-start(f32[1,8,16,512]{3,2,1,0:T(8,128)} %tr_ref.1) | copy-start | bytes 786436
where the time goes:
time: 47.6 us; the launch traced here: 47.4 us
  Pallas kernels  41.4 us (87%)
  local copies, waits for them, and re-layouts  4.69 us (10%)
  between operations  1.3 us (3%)
    pallas_call x1, Pallas kernels, on_device_pair(): pl.pallas_call(functools.partial(kernel, n_in, n_tm), out_shape=(jax.Shap...  41.4 us
    unnamed x7, local copies, waits for them, and re-layouts  4.69 us

commit v1 on v0

--- a/solution.py
+++ b/solution.py
@@ -122,9 +122,9 @@
 
 def kernel(
     n_in, n_tm,
-    cls_ref, tr_ref, st_ref, w_ref, mig_ref, res_ref,
+    cls_ref, tr_ref, st_hbm, w_hbm, mig_ref, res_ref,
     vt, p0, p1, ext, prev_strip, next_strip, img, bh, bl, cl, sa, sb, mg, px,
-    local_sem, send_sem, recv_sem,
+    st_ref, w_ref, spare, local_sem, send_sem, recv_sem,
 ):
     o = lax.axis_index("offset")
     i = lax.axis_index("inline")
@@ -139,6 +139,12 @@
     plane = 2 * n_tm
     m = o * n_tm + t
 
+    start_copy = pltpu.make_async_copy(st_hbm, st_ref, local_sem.at[0])
+    weight_copy = pltpu.make_async_copy(w_hbm, w_ref, local_sem.at[1])
+    own_copy = pltpu.make_async_copy(tr_ref.at[0, :, own_x], vt.at[0, pl.ds(APER, rows)], local_sem.at[2])
+    spare_copy = pltpu.make_async_copy(tr_ref.at[0, :, other_x], spare, local_sem.at[3])
+    local_copies = (start_copy, weight_copy, own_copy, spare_copy)
+
     barrier = pltpu.get_barrier_semaphore()
     greeted = []
     for d in range(1, plane):
@@ -152,6 +158,8 @@
             greeted.append((o, lax.rem(i + di, n_in), lax.rem(t + dt, n_tm)))
     for device in greeted:
         pl.semaphore_signal(barrier, inc=1, device_id=device, device_id_type=MESH)
+    for copy in local_copies:
+        copy.start()
     pl.semaphore_wait(barrier, len(greeted))
 
     used = [0]
@@ -219,8 +227,6 @@
         entry.append(neighbour(tr_ref.at[0, pl.ds(0, APER), xs], vt.at[slot, hi_halo], -1, 0, slot))
         entry.append(neighbour(tr_ref.at[0, pl.ds(rows - APER, APER), xs], vt.at[slot, lo_halo], 1, 0, slot))
     entry.append(send(tr_ref.at[0, :, other_x], vt.at[1, body], (other, i, t)))
-    own_copy = pltpu.make_async_copy(tr_ref.at[0, :, own_x], vt.at[0, body], local_sem)
-    own_copy.start()
 
     @pl.when(i == 0)
     def _():
@@ -272,7 +278,7 @@
     groups = lax.broadcasted_iota(jnp.int32, (2 * TB // K, K, TB), 0)
 
     def build(slot):
-        masks = [cl[slot] == c for c in range(st_ref.shape[0])]
+        masks = [cl[slot] == c for c in range(st_ref.shape[1])]
 
         def one(j, carry):
             cols = pl.ds(pl.multiple_of(j * TB, TB), TB)
@@ -280,7 +286,7 @@
                 start = jnp.zeros((K, TB), jnp.int32)
                 taps = jnp.zeros((K, TB), jnp.float32)
                 for c, mask in enumerate(masks):
-                    row = jnp.broadcast_to(st_ref[c, a:a + 1, cols], (K, TB))
+                    row = jnp.broadcast_to(st_ref[a, c:c + 1, cols], (K, TB))
                     start = jnp.where(mask, row, start)
                     taps = jnp.where(mask, w_ref[c, a, :, cols], taps)
                 reach = lane + LAG - start - sub
@@ -299,6 +305,8 @@
 
         lax.fori_loop(0, tiles, one, 0)
 
+    start_copy.wait()
+    weight_copy.wait()
     build(0)
     class_msg.received()
     build(1)
@@ -371,7 +379,8 @@
 
     def start_total(turn, parts):
         for n, part in enumerate(parts):
-            sa[turn, m, n] = part
+            sa[turn, m, n:n + 1] = jnp.sum(part, axis=0, keepdims=True)
+        sa[turn, m, len(parts):] = jnp.zeros((K - len(parts), TB), jnp.float32)
         messages = []
         for d in range(1, plane):
             peer = lax.rem(m + d, plane)
@@ -392,10 +401,8 @@
         for message in messages:
             message.received()
         total = sum(sb[turn, s] for s in range(n_in))
-        return [
-            jnp.sum(jnp.sum(total[n], axis=1, keepdims=True), axis=0, keepdims=True)
-            for n in range(total.shape[0])
-        ]
+        total = jnp.sum(total, axis=1, keepdims=True)
+        return [total[n:n + 1] for n in range(3)]
 
     def own_image(u):
         return img[u, APER:APER + rows, :, LAG:]
@@ -416,8 +423,7 @@
         neighbour(p0.at[:, last_rows], p0.at[:, lo_halo], 1, 0),
     ]
     own_p0 = p0[:, APER:APER + rows]
-    zero_tile = jnp.zeros((xl, TB), jnp.float32)
-    messages = start_total(0, [tile_sum(own_image(0) * own_image(0)), tile_sum(own_p0 * own_p0), zero_tile])
+    messages = start_total(0, [tile_sum(own_image(0) * own_image(0)), tile_sum(own_p0 * own_p0)])
     px0_msg = send(p0.at[1, body], px.at[0], (other, i, t))
     for message in halo:
         message.received()
@@ -433,13 +439,21 @@
     def store_p1(j, part):
         for slot in range(2):
             p1[slot, :, :, j * TB:(j + 1) * TB] = part[:, :, slot * TB:(slot + 1) * TB]
+        if j < tiles - 1:
+            send_p1(j)
+
+    px1_msgs = []
+
+    def send_p1(j):
+        cols = pl.ds(j * TB, TB)
+        px1_msgs.append(send(p1.at[1, :, :, cols], px.at[1, :, :, cols], (other, i, t)))
 
     demigrate(1, store_p1)
-    px1_msg = send(p1.at[1], px.at[1], (other, i, t))
     own_p0 = p0[:, APER:APER + rows]
     own_p1 = p1[...]
     messages = start_total(1, [
         tile_sum(own_image(1) * own_image(1)), tile_sum(own_p1 * own_p1), tile_sum(own_p1 * own_p0)])
+    send_p1(tiles - 1)
     messages = next_total(1, messages)
     gnew, square, cross = end_total(1, messages)
     beta = gnew / gnorm
@@ -453,11 +467,12 @@
         return r0 - step0 * a0 - step1 * (a1 + beta * a0)
 
     mig_ref[:, own_x, :] = image_of(own_image(0), own_image(1))
-    res_ref[0, :, own_x, :] = residual_of(tr_ref[0, :, own_x, :], p0[0, APER:APER + rows], p1[0])
-    for message in (mg0_msg, px0_msg, mg1_msg, px1_msg):
+    res_ref[0, :, own_x, :] = residual_of(vt[0, APER:APER + rows], p0[0, APER:APER + rows], p1[0])
+    spare_copy.wait()
+    for message in (mg0_msg, px0_msg, mg1_msg, *px1_msgs):
         message.received()
     mig_ref[:, other_x, :] = image_of(mg[0], mg[1])
-    res_ref[0, :, other_x, :] = residual_of(tr_ref[0, :, other_x, :], px[0], px[1])
+    res_ref[0, :, other_x, :] = residual_of(spare[...], px[0], px[1])
     for message in pending:
         message.sent()
 
@@ -470,13 +485,14 @@
     messages = 64
     f32 = jnp.float32
     vmem = pl.BlockSpec(memory_space=pltpu.VMEM)
+    hbm = pl.BlockSpec(memory_space=pltpu.HBM)
     return pl.pallas_call(
         functools.partial(kernel, n_in, n_tm),
         out_shape=(
             jax.ShapeDtypeStruct((rows, crosslines, window), f32),
             jax.ShapeDtypeStruct((1, rows, crosslines, window), f32),
         ),
-        in_specs=[pl.BlockSpec(memory_space=pltpu.SMEM), vmem, vmem, vmem],
+        in_specs=[pl.BlockSpec(memory_space=pltpu.SMEM), hbm, hbm, hbm],
         out_specs=(vmem, vmem),
         scratch_shapes=[
             pltpu.VMEM((2, wide, xl, window), f32),
@@ -489,18 +505,21 @@
             pltpu.VMEM((NAPER, tiles, 2 * TB, 2 * TB), jnp.bfloat16),
             pltpu.VMEM((NAPER, tiles, 2 * TB, 2 * TB), jnp.bfloat16),
             pltpu.VMEM((2, K, TB), jnp.int32),
-            pltpu.VMEM((2, 2 * n_tm, 3, xl, TB), f32),
-            pltpu.VMEM((2, n_in, 3, xl, TB), f32),
+            pltpu.VMEM((2, 2 * n_tm, K, TB), f32),
+            pltpu.VMEM((2, n_in, K, TB), f32),
             pltpu.VMEM((2, rows, xl, window), f32),
             pltpu.VMEM((2, rows, xl, window), f32),
-            pltpu.SemaphoreType.DMA,
+            pltpu.VMEM((NAPER,) + band_start.shape[:1] + (window,), jnp.int32),
+            pltpu.VMEM(band_weights.shape, f32),
+            pltpu.VMEM((rows, xl, window), f32),
+            pltpu.SemaphoreType.DMA((4,)),
             pltpu.SemaphoreType.DMA((messages,)),
             pltpu.SemaphoreType.DMA((messages,)),
         ],
         compiler_params=pltpu.CompilerParams(
-            collective_id=0, has_side_effects=True, vmem_limit_bytes=40 * 1024 * 1024
+            collective_id=0, has_side_effects=True, vmem_limit_bytes=60 * 1024 * 1024
         ),
-    )(class_of_block, traces, band_start, band_weights)
+    )(class_of_block, traces, band_start.transpose(1, 0, 2), band_weights)
 
 
 def solution(mesh):

time: 47.6 us -> 46 us (0.966)
  local copies, waits for them, and re-layouts: 4.69 us -> 3.34 us
    unnamed x7 -> x2, local copies, waits for them, and re-layouts: 4.69 us -> 3.34 us
where the time goes in v1:
time: 46 us; the launch traced here: 45.8 us
  Pallas kernels  41.2 us (90%)
  local copies, waits for them, and re-layouts  3.34 us (7%)
  between operations  1.28 us (3%)
    pallas_call x1, Pallas kernels, on_device_pair(): pl.pallas_call(functools.partial(kernel, n_in, n_tm), out_shape=(jax.Shap...  41.2 us
    unnamed x2, local copies, waits for them, and re-layouts  3.34 us

profile of v1, /device:TPU:0, one launch (start us, length us, event | category | flops | bytes accessed | tf_op | source)
XLA Modules:
  0.0 45.8 jit_solution(10135704822354165920)
XLA Ops:
  1.3 41.2 %shard_map.59 = (f32[8,16,512]{2,1,0:T(8,128)}, f32[1,8,16,512]{3,2,1,0:T(8,128)}) custom-call(s32[1]{0:T(128)S(6)} %copy.8.cls_ref, f32[1,8,16,512]{3,2,1,0:T(8,128)} %tr_ref.1, s32[5,16,512]{2,1,0:T(8,128)} %bitcast.1, f32[16,5,8,512]{3,2,1,0:T(8,128)} %w_hbm.1), custom_call_target="tpu_custom_call" | custom-call | tf_op jit(solution)/shard_map/pallas_call | solution.py:489
  42.5 1.7 %copy.9 = f32[8,16,512]{2,1,0:T(8,128)} copy(f32[8,16,512]{2,1,0:T(8,128)} %get-tuple-element.4) | data formatting | bytes 524288
  44.1 1.7 %copy.10 = f32[1,8,16,512]{3,2,1,0:T(8,128)} copy(f32[1,8,16,512]{3,2,1,0:T(8,128)} %get-tuple-element.5) | data formatting | bytes 524288

commit v2 on v1

--- a/solution.py
+++ b/solution.py
@@ -222,11 +222,19 @@
 
     cl[0] = jnp.full(cl.shape[1:], cls_ref[0], jnp.int32)
     class_msg = send(cl.at[0], cl.at[1], (other, i, t))
-    entry = []
-    for slot, xs in ((1, other_x), (0, own_x)):
-        entry.append(neighbour(tr_ref.at[0, pl.ds(0, APER), xs], vt.at[slot, hi_halo], -1, 0, slot))
-        entry.append(neighbour(tr_ref.at[0, pl.ds(rows - APER, APER), xs], vt.at[slot, lo_halo], 1, 0, slot))
-    entry.append(send(tr_ref.at[0, :, other_x], vt.at[1, body], (other, i, t)))
+    entry = {}
+    part = max(1, tiles // 2) * TB
+    for begin in range(0, window, part):
+        piece = pl.ds(begin, min(part, window - begin))
+        arriving = entry[begin // TB] = []
+        for slot, xs in ((1, other_x), (0, own_x)):
+            arriving.append(neighbour(
+                tr_ref.at[0, pl.ds(0, APER), xs, piece], vt.at[slot, hi_halo, :, piece], -1, 0, slot))
+            arriving.append(neighbour(
+                tr_ref.at[0, pl.ds(rows - APER, APER), xs, piece],
+                vt.at[slot, lo_halo, :, piece], 1, 0, slot))
+        arriving.append(send(
+            tr_ref.at[0, :, other_x, piece], vt.at[1, body, :, piece], (other, i, t)))
 
     @pl.when(i == 0)
     def _():
@@ -311,8 +319,6 @@
     class_msg.received()
     build(1)
     own_copy.wait()
-    for message in entry:
-        message.received()
 
     def apply(data, firsts, j, dims):
         high = data.astype(jnp.bfloat16).astype(jnp.float32)
@@ -331,10 +337,12 @@
             total = term if total is None else total + term
         return total
 
-    def migrate(values, u):
+    def migrate(values, u, arrivals):
         carried = None
         for j in range(tiles):
             cols = slice(j * TB, (j + 1) * TB)
+            for message in arrivals.get(j, ()):
+                message.received()
             data = jnp.concatenate([values[0, :, :, cols], values[1, :, :, cols]], axis=2)
             part = apply(data, [2 * APER - a for a in range(NAPER)], j, (((1,), (1,)), ((), ())))
             head = part[:, :TB] if carried is None else part[:, :TB] + carried
@@ -360,8 +368,7 @@
             ext.at[u, body, :, pl.ds(0, TB)], next_strip.at[u, body], 0, -1))
         messages.append(neighbour(
             ext.at[u, body, :, pl.ds(window, TB)], prev_strip.at[u, body], 0, 1))
-        for message in messages:
-            message.received()
+        return messages
 
     def whole(u):
         earlier = ext[u, :, :, :TB] + prev_strip[u]
@@ -407,8 +414,9 @@
     def own_image(u):
         return img[u, APER:APER + rows, :, LAG:]
 
-    migrate(vt, 0)
-    swap_edges(0)
+    migrate(vt, 0, entry)
+    for message in swap_edges(0):
+        message.received()
     for cols, value in whole(0):
         img[0, :, :, cols] = value
     mg0_msg = send(img.at[0, body, :, pl.ds(LAG, window)], mg.at[0], (other, i, t))
@@ -417,19 +425,22 @@
         for slot in range(2):
             p0[slot, APER:APER + rows, :, j * TB:(j + 1) * TB] = part[:, :, slot * TB:(slot + 1) * TB]
 
+        cols = pl.ds(j * TB, TB)
+        halo[j] = [
+            neighbour(p0.at[:, first_rows, :, cols], p0.at[:, hi_halo, :, cols], -1, 0),
+            neighbour(p0.at[:, last_rows, :, cols], p0.at[:, lo_halo, :, cols], 1, 0),
+        ]
+
+    halo = {}
     demigrate(0, store_p0)
-    halo = [
-        neighbour(p0.at[:, first_rows], p0.at[:, hi_halo], -1, 0),
-        neighbour(p0.at[:, last_rows], p0.at[:, lo_halo], 1, 0),
-    ]
     own_p0 = p0[:, APER:APER + rows]
     messages = start_total(0, [tile_sum(own_image(0) * own_image(0)), tile_sum(own_p0 * own_p0)])
     px0_msg = send(p0.at[1, body], px.at[0], (other, i, t))
-    for message in halo:
+    migrate(p0, 1, halo)
+    edges = swap_edges(1)
+    messages = next_total(0, messages)
+    for message in edges:
         message.received()
-    messages = next_total(0, messages)
-    migrate(p0, 1)
-    swap_edges(1)
     gnorm, curvature, _ = end_total(0, messages)
     step0 = gnorm / curvature
     for cols, value in whole(1):
@@ -439,21 +450,13 @@
     def store_p1(j, part):
         for slot in range(2):
             p1[slot, :, :, j * TB:(j + 1) * TB] = part[:, :, slot * TB:(slot + 1) * TB]
-        if j < tiles - 1:
-            send_p1(j)
-
-    px1_msgs = []
-
-    def send_p1(j):
-        cols = pl.ds(j * TB, TB)
-        px1_msgs.append(send(p1.at[1, :, :, cols], px.at[1, :, :, cols], (other, i, t)))
 
     demigrate(1, store_p1)
     own_p0 = p0[:, APER:APER + rows]
     own_p1 = p1[...]
     messages = start_total(1, [
         tile_sum(own_image(1) * own_image(1)), tile_sum(own_p1 * own_p1), tile_sum(own_p1 * own_p0)])
-    send_p1(tiles - 1)
+    px1_msg = send(p1.at[1], px.at[1], (other, i, t))
     messages = next_total(1, messages)
     gnew, square, cross = end_total(1, messages)
     beta = gnew / gnorm
@@ -469,7 +472,7 @@
     mig_ref[:, own_x, :] = image_of(own_image(0), own_image(1))
     res_ref[0, :, own_x, :] = residual_of(vt[0, APER:APER + rows], p0[0, APER:APER + rows], p1[0])
     spare_copy.wait()
-    for message in (mg0_msg, px0_msg, mg1_msg, *px1_msgs):
+    for message in (mg0_msg, px0_msg, mg1_msg, px1_msg):
         message.received()
     mig_ref[:, other_x, :] = image_of(mg[0], mg[1])
     res_ref[0, :, other_x, :] = residual_of(spare[...], px[0], px[1])
@@ -482,7 +485,7 @@
     xl = crosslines // 2
     wide = rows + 2 * APER
     tiles = window // TB
-    messages = 64
+    messages = 96
     f32 = jnp.float32
     vmem = pl.BlockSpec(memory_space=pltpu.VMEM)
     hbm = pl.BlockSpec(memory_space=pltpu.HBM)

time: 46 us -> 43.7 us (0.950)
  Pallas kernels: 41.2 us -> 38.9 us
    pallas_call x1, Pallas kernels: 41.2 us -> 38.9 us  [on_device_pair(): pl.pallas_call(functools.partial(kernel, n_in, n_tm), out_shape=(jax.Shap...]
where the time goes in v2:
time: 43.7 us; the launch traced here: 43.5 us
  Pallas kernels  38.9 us (89%)
  local copies, waits for them, and re-layouts  3.34 us (8%)
  between operations  1.28 us (3%)
    pallas_call x1, Pallas kernels, on_device_pair(): pl.pallas_call(functools.partial(kernel, n_in, n_tm), out_shape=(jax.Shap...  38.9 us
    unnamed x2, local copies, waits for them, and re-layouts  3.34 us

profile of v2, /device:TPU:0, one launch (start us, length us, event | category | flops | bytes accessed | tf_op | source)
XLA Modules:
  0.0 43.5 jit_solution(4466403705625084969)
XLA Ops:
  1.3 38.9 %shard_map.59 = (f32[8,16,512]{2,1,0:T(8,128)}, f32[1,8,16,512]{3,2,1,0:T(8,128)}) custom-call(s32[1]{0:T(128)S(6)} %copy.8.cls_ref, f32[1,8,16,512]{3,2,1,0:T(8,128)} %tr_ref.1, s32[5,16,512]{2,1,0:T(8,128)} %bitcast.1, f32[16,5,8,512]{3,2,1,0:T(8,128)} %w_hbm.1), custom_call_target="tpu_custom_call" | custom-call | tf_op jit(solution)/shard_map/pallas_call | solution.py:492
  40.2 1.7 %copy.9 = f32[8,16,512]{2,1,0:T(8,128)} copy(f32[8,16,512]{2,1,0:T(8,128)} %get-tuple-element.4) | data formatting | bytes 524288
  41.9 1.7 %copy.10 = f32[1,8,16,512]{3,2,1,0:T(8,128)} copy(f32[1,8,16,512]{3,2,1,0:T(8,128)} %get-tuple-element.5) | data formatting | bytes 524288

commit v3 on v2

--- a/solution.py
+++ b/solution.py
@@ -445,7 +445,6 @@
     step0 = gnorm / curvature
     for cols, value in whole(1):
         img[1, :, :, cols] = img[0, :, :, cols] - step0[None] * value
-    mg1_msg = send(img.at[1, body, :, pl.ds(LAG, window)], mg.at[1], (other, i, t))
 
     def store_p1(j, part):
         for slot in range(2):
@@ -456,6 +455,7 @@
     own_p1 = p1[...]
     messages = start_total(1, [
         tile_sum(own_image(1) * own_image(1)), tile_sum(own_p1 * own_p1), tile_sum(own_p1 * own_p0)])
+    mg1_msg = send(img.at[1, body, :, pl.ds(LAG, window)], mg.at[1], (other, i, t))
     px1_msg = send(p1.at[1], px.at[1], (other, i, t))
     messages = next_total(1, messages)
     gnew, square, cross = end_total(1, messages)

time: 43.7 us -> 41.9 us (0.959)
  Pallas kernels: 38.9 us -> 37.1 us
    pallas_call x1, Pallas kernels: 38.9 us -> 37.1 us  [on_device_pair(): pl.pallas_call(functools.partial(kernel, n_in, n_tm), out_shape=(jax.Shap...]
where the time goes in v3:
time: 41.9 us; the launch traced here: 41.8 us
  Pallas kernels  37.1 us (89%)
  local copies, waits for them, and re-layouts  3.34 us (8%)
  between operations  1.28 us (3%)
    pallas_call x1, Pallas kernels, on_device_pair(): pl.pallas_call(functools.partial(kernel, n_in, n_tm), out_shape=(jax.Shap...  37.1 us
    unnamed x2, local copies, waits for them, and re-layouts  3.34 us

profile of v3, /device:TPU:0, one launch (start us, length us, event | category | flops | bytes accessed | tf_op | source)
XLA Modules:
  0.0 41.8 jit_solution(6620422064854533927)
XLA Ops:
  1.3 37.1 %shard_map.59 = (f32[8,16,512]{2,1,0:T(8,128)}, f32[1,8,16,512]{3,2,1,0:T(8,128)}) custom-call(s32[1]{0:T(128)S(6)} %copy.8.cls_ref, f32[1,8,16,512]{3,2,1,0:T(8,128)} %tr_ref.1, s32[5,16,512]{2,1,0:T(8,128)} %bitcast.1, f32[16,5,8,512]{3,2,1,0:T(8,128)} %w_hbm.1), custom_call_target="tpu_custom_call" | custom-call | tf_op jit(solution)/shard_map/pallas_call | solution.py:492
  38.4 1.7 %copy.9 = f32[8,16,512]{2,1,0:T(8,128)} copy(f32[8,16,512]{2,1,0:T(8,128)} %get-tuple-element.4) | data formatting | bytes 524288
  40.1 1.7 %copy.10 = f32[1,8,16,512]{3,2,1,0:T(8,128)} copy(f32[1,8,16,512]{3,2,1,0:T(8,128)} %get-tuple-element.5) | data formatting | bytes 524288
